TPU v7x, 32 devices: a whole 2x2x4 slice. The times are simulated.
32 devices in a mesh: runs: 2 (over y), tm: 16 (over z, x, core).
Axes of the slice: x: 2, y: 2, z: 4, core: 2. Of those that a mesh axis runs over, the one named last changes fastest.
Arguments:
- frames: float32 [32, 64, 2048], P(('runs', 'tm')), parts along dimension 0, may hold values from -12 to 12
- validity: int32 [32, 128], P(('runs', 'tm')), parts along dimension 0, may hold values 0 or 1
- anchors: int32 [4], P('runs'), parts along dimension 0, may hold values from 0 to 31
Outputs:
- planes: float32 [8, 32, 32, 128], P('runs', None, None, 'tm'), parts along dimension 0
There are 2 independent parts, one for each index of `runs`. A program takes and returns all parts, laid end to end along the dimension named above; each array names one. Nothing has to cross between parts.
All inputs are finite; a program needn't handle non-finite values. No bound on the sum of `validity` on one device may be relied on, other than what follows from the above.
Results may differ from a plain program's by a relative error of at most 0.0003.
Values sent between devices are 32-bit elements; how exact they have to be, the bound alone decides.
A program may use at most 128 MiB of HBM per device.

v0:
```python
import math

import jax
import jax.numpy as jnp
from jax import lax
from jax.sharding import PartitionSpec as P

WIN = 64


PRECISE = lax.Precision.HIGHEST
DISTANCES = (1, 2, 4, 8)


def shifted_2(block, axis, distance):
    devices = range(lax.axis_size(axis))
    route = [(i - distance, i) for i in devices if i - distance in devices]
    return lax.ppermute(block, axis, route)


def tables(window, lag_count):
    grid = jnp.arange(window, dtype=jnp.int32)
    phase = grid[:, None] * grid[None, :] % window
    angle = phase.astype(jnp.float32) * (2.0 * math.pi / window)
    cosine = jnp.cos(angle)
    minus_sine = -jnp.sin(angle)
    first_table = jnp.stack([cosine, minus_sine], axis=1)
    second_table = jnp.stack(
        [jnp.stack([cosine, -minus_sine], axis=-1), jnp.stack([minus_sine, cosine], axis=-1)],
        axis=1,
    )
    shifted = (jnp.arange(lag_count, dtype=jnp.int32) - window // 4) % window
    back_phase = shifted[:, None] * grid[None, :] % window
    back_angle = back_phase.astype(jnp.float32) * (2.0 * math.pi / window)
    back_cos = jnp.cos(back_angle)
    back_sin = jnp.sin(back_angle)
    third_table = jnp.stack(
        [jnp.stack([back_cos.T, back_sin.T], axis=1), jnp.stack([-back_sin.T, back_cos.T], axis=1)],
        axis=0,
    )
    fourth_table = jnp.stack([back_cos, -back_sin], axis=-1)
    return (first_table, second_table, third_table, fourth_table)


def cut_windows(padded, row_start, col_start, block_rows, window, columns):
    stride = window // 2
    across = columns // stride
    region = lax.dynamic_slice(
        padded, (row_start, col_start), (stride * (block_rows + 1), columns + stride)
    )
    pieces = region.reshape(block_rows + 1, stride, across + 1, stride)
    stacked = jnp.concatenate([pieces[:-1], pieces[1:]], axis=1)
    joined = jnp.concatenate([stacked[:, :, :-1], stacked[:, :, 1:]], axis=3)
    windows = joined.transpose(1, 3, 0, 2).reshape(window, window, block_rows * across)
    return windows - jnp.mean(windows, axis=(0, 1), keepdims=True)


def spectrum(windows, first_table, second_table):
    half = jnp.einsum("ijr,jck->ickr", windows, first_table, precision=PRECISE)
    return jnp.einsum("pdic,ickr->pdkr", second_table, half, precision=PRECISE)


def cross_of(own_spectrum, later_spectrum, weight):
    own_real = own_spectrum[:, 0]
    own_imag = own_spectrum[:, 1]
    late_real = later_spectrum[:, 0]
    late_imag = later_spectrum[:, 1]
    cross_real = (own_real * late_real + own_imag * late_imag) * weight
    cross_imag = (own_real * late_imag - own_imag * late_real) * weight
    return jnp.stack([cross_real, cross_imag], axis=1)


def back_transform(cross, third_table, fourth_table):
    middle = jnp.einsum("pckr,ckdv->pdvr", cross, third_table, precision=PRECISE)
    return jnp.einsum("pdvr,upd->uvr", middle, fourth_table, precision=PRECISE)


def body(frames, validity, anchors):
    current = frames[0]
    pixel_rows, columns = current.shape
    window = WIN
    stride = window // 2
    window_rows = pixel_rows // stride
    lag_count = window // 2
    total_frames = lax.axis_size("tm")
    position = lax.axis_index("tm")
    first_table, second_table, third_table, fourth_table = tables(window, lag_count)
    own_valid = validity[0].astype(jnp.float32)
    padded_own = jnp.pad(current, ((0, 2 * stride), (0, 2 * stride)))
    windows = cut_windows(padded_own, anchors[0], anchors[1], window_rows, window, columns)
    own_spectrum = spectrum(windows, first_table, second_table)
    results = []
    for distance in DISTANCES:
        partner, partner_valid = shifted_2((own_spectrum, own_valid), "tm", -distance)
        later_index = position + distance
        inside = (later_index < total_frames).astype(jnp.float32)
        scale = 1.0 / (float(total_frames - distance) * float(window) ** 4)
        weight = own_valid * partner_valid * inside * scale
        results.append(
            back_transform(cross_of(own_spectrum, partner, weight), third_table, fourth_table)
        )
    partial_value = jnp.stack(results)
    return lax.psum_scatter(partial_value, "tm", scatter_dimension=3, tiled=True)


def solution(mesh):
    placed = (P(("runs", "tm"), None, None), P(("runs", "tm"), None), P("runs"))
    return jax.shard_map(
        body, mesh=mesh, in_specs=placed, out_specs=P("runs", None, None, "tm"), check_vma=False
    )
```

profile of v0, /device:TPU:0, one launch (start us, length us, event | category | flops | bytes accessed | tf_op | source)
XLA Modules:
  0.0 632.8 jit_solution(2301412530091748642)
XLA Ops:
  13.1 2.1 pad_dynamic-slice_fusion
  16.8 2.9 slice.65
  19.8 2.1 copy.9
  23.6 5.8 copy.10
  29.4 4.3 reshape.405
  33.8 3.5 convolution_bitcast_fusion
  37.3 9.4 %fusion.17 = f32[64,2,64,128]{3,0,2,1:T(8,128)} fusion(f32[64,2,64,128]{3,2,0,1:T(8,128)S(1)} %convolution_bitcast_fusion, f32[64,1,64,2]{2,0,3,1:T(8,128)S(1)} %get-tuple-element.20, f32[64,1,64,2]{2,0,3,1:T(8,128)S(1)} %get-tuple-element.19), kind=kOutput, calls=%fused_computation.22 | convolution fusion | flops 1610629120 | bytes 8454144 | tf_op jit(solution)/shard_map/pdic,ickr->pdkr/dot_general | solution.py:60
  53.6 403.9 %collective-permute-done.7 = f32[128]{0:T(128)S(1)} collective-permute-done((f32[128]{0:T(128)S(1)}, f32[128]{0:T(128)S(1)}, u32[]{:S(2)}, u32[]{:S(2)}) %collective-permute-start.7) | collective-permute-done | bytes 544 | tf_op jit(solution)/shard_map/ppermute | solution.py:18
  458.8 4.1 collective-permute-done.3
  464.2 4.1 collective-permute-done.5
  469.6 1.7 collective-permute-done.1
  471.4 5.4 add_multiply_fusion.1
  477.7 4.8 fusion.36
  482.5 4.8 fusion.39
  487.2 2.5 fusion.48
  489.8 2.3 fusion.51
  492.1 5.4 add_multiply_fusion.3
  497.8 4.8 fusion.30
  502.6 2.3 fusion.42
  505.2 5.0 fusion.33
  510.2 2.3 fusion.45
  512.8 7.6 %copy.20 = f32[4,32,32,128]{2,1,0,3:T(8,128)} copy(f32[4,32,32,128]{3,1,2,0:T(8,128)S(1)} %pad_maximum_fusion.5) | data formatting | bytes 4194304 | tf_op jit(solution)/shard_map/stack | solution.py:102
  520.4 103.3 %reduce-scatter.2.cloned.1.call-done = f32[4,32,32,8]{2,1,0,3:T(8,128)} async-done(((f32[4,32,32,128]{2,1,0,3:T(8,128)}), f32[4,32,32,8]{2,1,0,3:T(8,128)}) %reduce-scatter.2.cloned.1.call-update) | async-done | bytes 131088 | tf_op jit(solution)/shard_map/reduce_scatter | solution.py:103
  623.6 2.1 copy.21
  (45 shorter events, 18.8 us)
Async XLA Ops:
  6.5 617.1 %reduce-scatter.2.cloned.1.call-start = ((), (), s32[]{:S(2)}) async-start(), calls=%async_computation.1 | async-start | bytes 8912896 | tf_op jit(solution)/shard_map/reduce_scatter | solution.py:103
  29.4 4.4 copy-start
  29.4 4.4 copy-start.1
  29.4 4.4 copy-start.2
  37.3 14.6 %copy-start.3 = (s32[1,128]{1,0:T(1,128)S(1)}, s32[1,128]{1,0:T(1,128)}, u32[]{:S(2)}) copy-start(s32[1,128]{1,0:T(1,128)} %param.4) | copy-start | bytes 1540
  46.8 424.6 %collective-permute-start.6 = (f32[64,2,64,128]{3,0,2,1:T(8,128)}, f32[64,2,64,128]{3,0,2,1:T(8,128)}, u32[]{:S(2)}, u32[]{:S(2)}) collective-permute-start(f32[64,2,64,128]{3,0,2,1:T(8,128)} %fusion.17), channel_id=1, source_target_pairs={{8,0},{9,1},{10,2},{11,3},{12,4},{13,5},{14,6},{15,7},{24,16},{25,... | collective-permute-start | bytes 12582920 | tf_op jit(solution)/shard_map/ppermute | solution.py:18
  48.1 423.3 %collective-permute-start.4 = (f32[64,2,64,128]{3,0,2,1:T(8,128)}, f32[64,2,64,128]{3,0,2,1:T(8,128)}, u32[]{:S(2)}, u32[]{:S(2)}) collective-permute-start(f32[64,2,64,128]{3,0,2,1:T(8,128)} %fusion.17), channel_id=1, source_target_pairs={{4,0},{5,1},{6,2},{7,3},{8,4},{9,5},{10,6},{11,7},{12,8},{13,9},{1... | collective-permute-start | bytes 12582920 | tf_op jit(solution)/shard_map/ppermute | solution.py:18
  49.4 442.7 %collective-permute-start.2 = (f32[64,2,64,128]{3,0,2,1:T(8,128)}, f32[64,2,64,128]{3,0,2,1:T(8,128)}, u32[]{:S(2)}, u32[]{:S(2)}) collective-permute-start(f32[64,2,64,128]{3,0,2,1:T(8,128)} %fusion.17), channel_id=1, source_target_pairs={{2,0},{3,1},{4,2},{5,3},{6,4},{7,5},{8,6},{9,7},{10,8},{11,9},{12,... | collective-permute-start | bytes 12582920 | tf_op jit(solution)/shard_map/ppermute | solution.py:18
  50.7 441.4 %collective-permute-start = (f32[64,2,64,128]{3,0,2,1:T(8,128)}, f32[64,2,64,128]{3,0,2,1:T(8,128)}, u32[]{:S(2)}, u32[]{:S(2)}) collective-permute-start(f32[64,2,64,128]{3,0,2,1:T(8,128)} %fusion.17), channel_id=1, source_target_pairs={{1,0},{2,1},{3,2},{4,3},{5,4},{6,5},{7,6},{8,7},{9,8},{10,9},{11,1... | collective-permute-start | bytes 12582920 | tf_op jit(solution)/shard_map/ppermute | solution.py:18
  52.0 405.5 %collective-permute-start.7 = (f32[128]{0:T(128)S(1)}, f32[128]{0:T(128)S(1)}, u32[]{:S(2)}, u32[]{:S(2)}) collective-permute-start(f32[128]{0:T(128)S(1)} %convert_bitcast_fusion), channel_id=1, source_target_pairs={{8,0},{9,1},{10,2},{11,3},{12,4},{13,5},{14,6},{15,7},{24,16},{25,... | collective-permute-start | bytes 1544 | tf_op jit(solution)/shard_map/ppermute | solution.py:18
  457.5 5.4 collective-permute-start.3
  462.9 5.4 collective-permute-start.5
  468.3 3.0 collective-permute-start.1
Sparse Core Ops, SparseCore 0:
  520.5 103.0 reduce-scatter.1
where the time goes:
time: 643 us; the launch traced here: 633 us
  waiting for transfers between devices  517 us (80%)
  matrix products  41.7 us (6%)
  local copies, waits for them, and re-layouts  29.9 us (5%)
  between operations  17.5 us (3%)
  other arithmetic  16.3 us (3%)
  starting transfers between devices  10.3 us (2%)
    ppermute x8, waiting for transfers between devices, shifted_2(): return lax.ppermute(block, axis, route)  414 us
    reduce_scatter x1, waiting for transfers between devices, body(): lax.psum_scatter(partial_value, 'tm', scatter_dimension=3, tiled=True)  103 us
    dot_general x4, matrix products, back_transform(): jnp.einsum('pckr,ckdv->pdvr', cross, third_table, precision=PRECISE)  19.3 us
  transfers between devices with their start and end apart: 9, of which 5 were waited for; matrix products, arithmetic and copies ran while one was open for 3% of the time, Pallas kernels for 0%

commit v1 on v0

--- a/solution.py
+++ b/solution.py
@@ -1,8 +1,13 @@
+import functools
 import math
 
 import jax
 import jax.numpy as jnp
+import ml_dtypes
+import numpy as np
 from jax import lax
+from jax.experimental import pallas as pl
+from jax.experimental.pallas import tpu as pltpu
 from jax.sharding import PartitionSpec as P
 
 WIN = 64
@@ -103,8 +108,271 @@
     return lax.psum_scatter(partial_value, "tm", scatter_dimension=3, tiled=True)
 
 
+GROUP = 16
+BF = jnp.bfloat16
+F32 = jnp.float32
+
+
+def halves(table):
+    table = table.astype(np.float32)
+    high = table.astype(ml_dtypes.bfloat16)
+    low = (table - high.astype(np.float32)).astype(ml_dtypes.bfloat16)
+    return high, low
+
+
+@functools.cache
+def constant_tables():
+    unit = 2.0 * np.pi / 64
+    cols = np.arange(160)[:, None]
+    wide = np.zeros((160, 384))
+    k = np.arange(32)[None, :]
+    for b in range(4):
+        inside = (cols >= 32 * b) & (cols < 32 * b + 64)
+        wide[:, 32 * b : 32 * b + 32] = np.cos(unit * (cols * k % 64)) * inside
+        wide[:, 128 + 32 * b : 160 + 32 * b] = -np.sin(unit * (cols * k % 64)) * inside
+        wide[:, 256 + b] = ((1 - 2 * (cols % 2)) * inside)[:, 0]
+    high, low = halves(wide)
+    w1 = np.concatenate([high[:128], high[:128]], axis=0)
+    w2 = np.concatenate(
+        [low[:128], high[128:], high[128:], low[128:], np.zeros_like(low[128:])], axis=0
+    )
+    p = np.arange(64)
+    angle = unit * (p[:, None] * p[None, :] % 64)
+    high, low = halves(np.concatenate([np.cos(angle), np.sin(angle)] * 2, axis=0))
+    m = np.concatenate([high, high, low], axis=1)
+    u = np.arange(32) - 16
+    angle = unit * (u[:, None] * p[None, :] % 64)
+    cosine, sine = np.cos(angle), np.sin(angle)
+    high, low = halves(
+        np.concatenate(
+            [np.concatenate([cosine, -sine], axis=1), np.concatenate([sine, cosine], axis=1)],
+            axis=0,
+        )
+    )
+    g = np.concatenate([high, high, low], axis=1)
+    back = np.zeros((384, 128))
+    twice = np.where(np.arange(32) == 0, 1.0, 2.0)[:, None]
+    angle = unit * (np.arange(32)[:, None] * u[None, :] % 64)
+    for b in range(4):
+        span = slice(32 * b, 32 * b + 32)
+        back[span, span] = twice * np.cos(angle)
+        back[128 + b, span] = 1 - 2 * (u % 2)
+        back[256 + 32 * b : 288 + 32 * b, span] = -twice * np.sin(angle)
+    high, low = halves(back)
+    h = np.concatenate([high, low], axis=1)
+    return w1, w2, m, g, h
+
+
+def column_block(device):
+    return lax.rem(device, 8) * 2 + device // 8
+
+
+def split(value):
+    high = value.astype(BF)
+    return high, (value - high.astype(F32)).astype(BF)
+
+
+def dot(left, right):
+    return jnp.dot(left, right, preferred_element_type=F32)
+
+
+def kernel(
+    anchor_ref, x_ref, v_ref, w1_ref, w2_ref, m_ref, g_ref, h_ref, out_ref,
+    pack, recv, mask_m, expand, sre, sim, cross, lag, plane,
+    send_sem, recv_sem, plane_send, plane_recv,
+):
+    me = lax.axis_index("tm")
+    side = me // 8
+    partner = lax.rem(me + 8, GROUP)
+    mine = column_block(me)
+
+    barrier = pltpu.get_barrier_semaphore()
+    for step in range(1, GROUP):
+        peer = lax.rem(me + step, GROUP)
+        pl.semaphore_signal(
+            barrier, inc=1, device_id={"tm": peer}, device_id_type=pl.DeviceIdType.MESH
+        )
+
+    row_start = anchor_ref[0]
+    col_start = anchor_ref[1]
+
+    lane = lax.broadcasted_iota(jnp.int32, (64, 128), 1)
+    lane16 = lax.broadcasted_iota(jnp.int32, (16, 128), 1)
+    keep = lane < 128 - col_start
+    amount = lax.rem(128 - col_start, 128)
+    valid_row = jnp.broadcast_to(v_ref[...].astype(F32), (8, 128))
+    following = jnp.zeros((64, 128), F32)
+    halo = jnp.zeros((16, 128), F32)
+    for block in reversed(range(GROUP)):
+        rolled = pltpu.roll(x_ref[:, 128 * block : 128 * block + 128], amount, 1)
+        shifted = jnp.where(keep, rolled, following)
+        pack[block, 0:64, :] = shifted
+        pack[block, 64:80, :] = halo
+        pack[block, 80:88, :] = valid_row
+        following = rolled
+        halo = shifted[0:16]
+        for group in range(1, 4):
+            moved = pltpu.roll(shifted[16 * group : 16 * group + 16], 32 * group, 1)
+            halo = jnp.where(lane16 >= 32 * group, moved, halo)
+
+    pl.semaphore_wait(barrier, GROUP - 1)
+
+    def transfer(source, target):
+        return pltpu.make_async_remote_copy(
+            src_ref=pack.at[column_block(target)],
+            dst_ref=recv.at[source],
+            send_sem=send_sem.at[target],
+            recv_sem=recv_sem.at[source],
+            device_id={"tm": target},
+            device_id_type=pl.DeviceIdType.MESH,
+        )
+
+    for step in range(1, GROUP):
+        transfer(me, lax.rem(me + step, GROUP)).start()
+
+    row = lax.rem(lax.broadcasted_iota(jnp.int32, (256, 192), 1), 64)
+    below = row_start + 32 * (lax.broadcasted_iota(jnp.int32, (256, 192), 0) // 128)
+    mask_m[...] = jnp.where(row >= below, m_ref[...].astype(F32), 0.0).astype(BF)
+    region = lax.broadcasted_iota(jnp.int32, (128, 512), 0)
+    place = lax.broadcasted_iota(jnp.int32, (128, 512), 1)
+    inner = lax.rem(place, 256)
+    which = jnp.where(inner < 128, inner // 32, inner - 128)
+    wanted = 64 * (place // 256) + 4 * mine + which
+    expand[...] = jnp.where((region == wanted) & (which < 4), 1.0, 0.0).astype(BF)
+
+    def spectra(t):
+        main_high, main_low = split(recv[t, 0:64, :])
+        edge = recv[t, 64:80, :]
+        edge_high = edge.astype(BF).astype(F32)
+        edge_low = edge - edge_high
+        tiles = []
+        for group in range(4):
+            first = pltpu.roll(edge_high, (128 - 32 * group) % 128, 1)
+            second = pltpu.roll(edge_low, (160 - 32 * group) % 128, 1)
+            third = pltpu.roll(edge_high, (192 - 32 * group) % 128, 1)
+            tile = jnp.where(lane16 < 32, first, jnp.where(lane16 < 64, second, third))
+            tiles.append(jnp.where(lane16 < 96, tile, 0.0))
+        edges = jnp.concatenate(tiles, axis=0).astype(BF)
+        half = dot(jnp.concatenate([main_high, main_low], axis=1), w1_ref[...])
+        half += dot(jnp.concatenate([main_high, edges], axis=1), w2_ref[...])
+        half_high, half_low = split(half)
+        full = dot(mask_m[...], jnp.concatenate([half_high, half_low, half_high], axis=0))
+        usable = dot(recv[t, 80:88, :].astype(BF), expand[...])[0:1, :]
+        for a in range(2):
+            cos_part = full[128 * a : 128 * a + 64]
+            sin_part = full[128 * a + 64 : 128 * a + 128]
+            weight = usable[:, 256 * a : 256 * a + 256]
+            sre[t, a, :, 0:128] = (cos_part[:, 0:128] + sin_part[:, 128:256]) * weight[:, 0:128]
+            sim[t, a, :, 0:128] = (cos_part[:, 128:256] - sin_part[:, 0:128]) * weight[:, 0:128]
+            sre[t, a, :, 128:256] = cos_part[:, 256:384] * weight[:, 128:256]
+            sim[t, a, :, 128:256] = -sin_part[:, 256:384] * weight[:, 128:256]
+
+    recv[me] = pack[mine]
+    spectra(me)
+
+    def arrive(step, carry):
+        source = lax.rem(me - step + GROUP, GROUP)
+        transfer(source, me).wait_recv()
+        spectra(source)
+        return carry
+
+    lax.fori_loop(1, GROUP, arrive, 0)
+
+    def correlate(index, carry):
+        a = index // 8
+        start = pl.multiple_of(lax.rem(index, 8) * 8, 8)
+        line = lax.broadcasted_iota(jnp.int32, (8, 128), 0) + start
+        column = lax.rem(lax.broadcasted_iota(jnp.int32, (8, 128), 1), 32)
+        for part in range(2):
+            lanes = slice(128 * part, 128 * part + 128)
+            real = [sre[t, a, pl.ds(start, 8), lanes] for t in range(GROUP)]
+            imag = [sim[t, a, pl.ds(start, 8), lanes] for t in range(GROUP)]
+            for e, distance in enumerate(DISTANCES):
+                total_real = jnp.zeros((8, 128), F32)
+                total_imag = jnp.zeros((8, 128), F32)
+                for t in range(GROUP - distance):
+                    later = t + distance
+                    total_real += real[t] * real[later] + imag[t] * imag[later]
+                    total_imag += real[t] * imag[later] - imag[t] * real[later]
+                scale = 1.0 / (float(GROUP - distance) * float(WIN) ** 4)
+                if part == 0:
+                    alive = (line > 0) | (column > 0)
+                    total_real = jnp.where(alive, total_real, 0.0)
+                    total_imag = jnp.where(alive, total_imag, 0.0)
+                cross[e, a, pl.ds(start, 8), lanes] = total_real * scale
+                cross[e, a, pl.ds(start + 64, 8), lanes] = total_imag * scale
+        return carry
+
+    lax.fori_loop(0, 16, correlate, 0)
+
+    def back(a):
+        for e in range(4):
+            high, low = split(cross[e, a])
+            middle = dot(g_ref[...], jnp.concatenate([high, low, high], axis=0))
+            lag[32 * e : 32 * e + 32, 0:256] = middle[0:32]
+            lag[32 * e : 32 * e + 32, 256:384] = middle[32:64, 0:128]
+        high, low = split(lag[...])
+        both = dot(high, h_ref[...])
+        return both[:, 0:128] + both[:, 128:256] + dot(low, h_ref[:, 0:128])
+
+    plane[...] = back(1 - side)
+    give = pltpu.make_async_remote_copy(
+        src_ref=plane,
+        dst_ref=out_ref.at[side],
+        send_sem=plane_send,
+        recv_sem=plane_recv,
+        device_id={"tm": partner},
+        device_id_type=pl.DeviceIdType.MESH,
+    )
+    give.start()
+    out_ref[side] = back(side)
+    for step in range(1, GROUP):
+        transfer(me, lax.rem(me + step, GROUP)).wait_send()
+    give.wait_send()
+    pltpu.make_async_remote_copy(
+        src_ref=plane,
+        dst_ref=out_ref.at[1 - side],
+        send_sem=plane_send,
+        recv_sem=plane_recv,
+        device_id={"tm": partner},
+        device_id_type=pl.DeviceIdType.MESH,
+    ).wait_recv()
+
+
+def group_body(frames, validity, anchors):
+    tables_in = [jnp.asarray(table) for table in constant_tables()]
+    vmem = pl.BlockSpec(memory_space=pltpu.VMEM)
+    halves_out = pl.pallas_call(
+        kernel,
+        out_shape=jax.ShapeDtypeStruct((2, 128, 128), F32),
+        in_specs=[pl.BlockSpec(memory_space=pltpu.SMEM)] + [vmem] * 7,
+        out_specs=vmem,
+        scratch_shapes=[
+            pltpu.VMEM((GROUP, 88, 128), F32),
+            pltpu.VMEM((GROUP, 88, 128), F32),
+            pltpu.VMEM((256, 192), BF),
+            pltpu.VMEM((128, 512), BF),
+            pltpu.VMEM((GROUP, 2, 64, 256), F32),
+            pltpu.VMEM((GROUP, 2, 64, 256), F32),
+            pltpu.VMEM((4, 2, 128, 256), F32),
+            pltpu.VMEM((128, 384), F32),
+            pltpu.VMEM((128, 128), F32),
+            pltpu.SemaphoreType.DMA((GROUP,)),
+            pltpu.SemaphoreType.DMA((GROUP,)),
+            pltpu.SemaphoreType.DMA,
+            pltpu.SemaphoreType.DMA,
+        ],
+        compiler_params=pltpu.CompilerParams(
+            collective_id=0, has_side_effects=True, vmem_limit_bytes=40 * 1024 * 1024
+        ),
+    )(anchors, frames[0], validity, *tables_in)
+    parts = halves_out.reshape(2, 4, 32, 4, 32)
+    return parts.transpose(1, 2, 4, 0, 3).reshape(4, 32, 32, 8)
+
+
 def solution(mesh):
     placed = (P(("runs", "tm"), None, None), P(("runs", "tm"), None), P("runs"))
+    chosen = group_body if mesh.shape["tm"] == GROUP else body
     return jax.shard_map(
-        body, mesh=mesh, in_specs=placed, out_specs=P("runs", None, None, "tm"), check_vma=False
-    )
+        chosen, mesh=mesh, in_specs=placed, out_specs=P("runs", None, None, "tm"), check_vma=False
+    )

time: 643 us -> 39 us (0.06)
  the two profiles are of different devices: /device:TPU:0 before, /device:TPU:12 now
where the time goes in v1:
time: 39 us; the launch traced here: 38.7 us
  Pallas kernels  31.4 us (81%)
  local copies, waits for them, and re-layouts  7.33 us (19%)
    pallas_call x1, Pallas kernels, group_body(): pl.pallas_call(kernel, out_shape=jax.ShapeDtypeStruct((2, 128, 128), F32)...  31.4 us
    unnamed x16, local copies, waits for them, and re-layouts  6.19 us
    transpose x1, local copies, waits for them, and re-layouts, group_body(): return parts.transpose(1, 2, 4, 0, 3).reshape(4, 32, 32, 8)  0.88 us

profile of v1, /device:TPU:12, one launch (start us, length us, event | category | flops | bytes accessed | tf_op | source)
XLA Modules:
  0.0 38.7 jit_solution(14541977894070759023)
XLA Ops:
  0.0 0.0 copy-start.6
  0.0 0.0 copy-start.7
  0.0 0.7 %copy-done.6 = s32[2]{0:T(128)S(1)} copy-done((s32[2]{0:T(128)S(1)}, s32[2]{0:T(128)}, u32[]{:S(2)}) %copy-start.6) | copy-done | bytes 32
  0.7 0.0 copy-done.7
  0.7 0.0 copy-start
  0.7 1.0 %copy-done = f32[1,64,2048]{2,1,0:T(8,128)S(1)} copy-done((f32[1,64,2048]{2,1,0:T(8,128)S(1)}, f32[1,64,2048]{2,1,0:T(8,128)}, u32[]{:S(2)}) %copy-start) | copy-done | bytes 524312
  1.7 0.0 copy-start.1
  1.7 0.9 %copy-done.1 = bf16[384,256]{1,0:T(8,128)(2,1)S(1)} copy-done((bf16[384,256]{1,0:T(8,128)(2,1)S(1)}, bf16[384,256]{1,0:T(8,128)(2,1)}, u32[]{:S(2)}) %copy-start.1) | copy-done | bytes 196632
  2.6 0.0 copy-start.2
  2.6 0.9 %copy-done.2 = bf16[256,384]{1,0:T(8,128)(2,1)S(1)} copy-done((bf16[256,384]{1,0:T(8,128)(2,1)S(1)}, bf16[256,384]{1,0:T(8,128)(2,1)}, u32[]{:S(2)}) %copy-start.2) | copy-done | bytes 196632
  3.6 0.0 copy-start.3
  3.6 0.9 %copy-done.3 = bf16[256,384]{1,0:T(8,128)(2,1)S(1)} copy-done((bf16[256,384]{1,0:T(8,128)(2,1)S(1)}, bf16[256,384]{1,0:T(8,128)(2,1)}, u32[]{:S(2)}) %copy-start.3) | copy-done | bytes 196632
  4.5 0.0 copy-start.4
  4.5 0.9 %copy-done.4 = bf16[256,192]{1,0:T(8,128)(2,1)S(1)} copy-done((bf16[256,192]{1,0:T(8,128)(2,1)S(1)}, bf16[256,192]{1,0:T(8,128)(2,1)}, u32[]{:S(2)}) %copy-start.4) | copy-done | bytes 98328
  5.4 0.0 copy-start.5
  5.4 0.8 %copy-done.5 = bf16[64,384]{1,0:T(8,128)(2,1)S(1)} copy-done((bf16[64,384]{1,0:T(8,128)(2,1)S(1)}, bf16[64,384]{1,0:T(8,128)(2,1)}, u32[]{:S(2)}) %copy-start.5) | copy-done | bytes 49176
  6.2 31.4 %shard_map.82 = f32[2,128,128]{2,1,0:T(8,128)S(1)} custom-call(s32[2]{0:T(128)S(1)} %copy-done.6, f32[64,2048]{1,0:T(8,128)S(1)} %bitcast.3, s32[1,128]{1,0:T(1,128)S(1)} %copy-done.7, bf16[256,384]{1,0:T(8,128)(2,1)S(1)} %copy-done.3, bf16[256,384]{1,0:T(8,128)(2,1)S(1)} %copy-done.2, bf16[256,192]{1,0:T(8,128)(2,1)S(1)} %copy-done.4, ...), custom_call_target="tpu_custom_call" | custom-call | tf_op jit(solution)/shard_map/pallas_call | solution.py:345
  37.6 0.3 reshape.6
  37.8 0.9 %copy.9 = f32[4,32,32,2,4]{2,4,3,1,0:T(4,128)} copy(f32[4,32,32,2,4]{2,4,1,0,3:T(4,128)S(1)} %bitcast.4) | data formatting | bytes 262144 | tf_op jit(solution)/shard_map/transpose | solution.py:370
Async XLA Ops:
  0.0 0.7 %copy-start.6 = (s32[2]{0:T(128)S(1)}, s32[2]{0:T(128)}, u32[]{:S(2)}) copy-start(s32[2]{0:T(128)} %anchor_ref.1) | copy-start | bytes 28
  0.0 0.7 %copy-start.7 = (s32[1,128]{1,0:T(1,128)S(1)}, s32[1,128]{1,0:T(1,128)}, u32[]{:S(2)}) copy-start(s32[1,128]{1,0:T(1,128)} %v_ref.1) | copy-start | bytes 1540
  0.7 1.0 %copy-start = (f32[1,64,2048]{2,1,0:T(8,128)S(1)}, f32[1,64,2048]{2,1,0:T(8,128)}, u32[]{:S(2)}) copy-start(f32[1,64,2048]{2,1,0:T(8,128)} %param.8) | copy-start | bytes 1572868
  1.7 0.9 %copy-start.1 = (bf16[384,256]{1,0:T(8,128)(2,1)S(1)}, bf16[384,256]{1,0:T(8,128)(2,1)}, u32[]{:S(2)}) copy-start(bf16[384,256]{1,0:T(8,128)(2,1)} %constant.14.clone.h_ref) | copy-start | bytes 589828
  2.6 0.9 %copy-start.2 = (bf16[256,384]{1,0:T(8,128)(2,1)S(1)}, bf16[256,384]{1,0:T(8,128)(2,1)}, u32[]{:S(2)}) copy-start(bf16[256,384]{1,0:T(8,128)(2,1)} %constant.11.clone.w2_ref) | copy-start | bytes 589828
  3.6 0.9 %copy-start.3 = (bf16[256,384]{1,0:T(8,128)(2,1)S(1)}, bf16[256,384]{1,0:T(8,128)(2,1)}, u32[]{:S(2)}) copy-start(bf16[256,384]{1,0:T(8,128)(2,1)} %constant.10.clone.w1_ref) | copy-start | bytes 589828
  4.5 0.9 %copy-start.4 = (bf16[256,192]{1,0:T(8,128)(2,1)S(1)}, bf16[256,192]{1,0:T(8,128)(2,1)}, u32[]{:S(2)}) copy-start(bf16[256,192]{1,0:T(8,128)(2,1)} %constant.12.clone.m_ref) | copy-start | bytes 294916
  5.4 0.8 %copy-start.5 = (bf16[64,384]{1,0:T(8,128)(2,1)S(1)}, bf16[64,384]{1,0:T(8,128)(2,1)}, u32[]{:S(2)}) copy-start(bf16[64,384]{1,0:T(8,128)(2,1)} %constant.13.clone.g_ref) | copy-start | bytes 147460

commit v2 on v1

--- a/solution.py
+++ b/solution.py
@@ -177,8 +177,8 @@
 
 
 def kernel(
-    anchor_ref, x_ref, v_ref, w1_ref, w2_ref, m_ref, g_ref, h_ref, out_ref,
-    pack, recv, mask_m, expand, sre, sim, cross, lag, plane,
+    anchor_hbm, x_hbm, v_hbm, w1_hbm, w2_hbm, m_hbm, g_hbm, h_hbm, out_ref,
+    anchor_ref, x_ref, v_ref, w1_ref, w2_ref, m_ref, g_ref, h_ref, load_sem, pack, recv, mask_m, expand, sre, sim, cross, lag, plane,
     send_sem, recv_sem, plane_send, plane_recv,
 ):
     me = lax.axis_index("tm")
@@ -193,6 +193,25 @@
             barrier, inc=1, device_id={"tm": peer}, device_id_type=pl.DeviceIdType.MESH
         )
 
+    loads = [
+        pltpu.make_async_copy(source, target, load_sem.at[index])
+        for index, (source, target) in enumerate(
+            [
+                (anchor_hbm, anchor_ref),
+                (x_hbm, x_ref),
+                (v_hbm, v_ref),
+                (m_hbm, m_ref),
+                (w1_hbm, w1_ref),
+                (w2_hbm, w2_ref),
+                (g_hbm, g_ref),
+                (h_hbm, h_ref),
+            ]
+        )
+    ]
+    for load in loads:
+        load.start()
+    for load in loads[:3]:
+        load.wait()
     row_start = anchor_ref[0]
     col_start = anchor_ref[1]
 
@@ -219,17 +238,21 @@
 
     def transfer(source, target):
         return pltpu.make_async_remote_copy(
-            src_ref=pack.at[column_block(target)],
-            dst_ref=recv.at[source],
+            src_ref=pack.at[column_block(target), pl.ds(0, 81)],
+            dst_ref=recv.at[source, pl.ds(0, 81)],
             send_sem=send_sem.at[target],
             recv_sem=recv_sem.at[source],
             device_id={"tm": target},
             device_id_type=pl.DeviceIdType.MESH,
         )
 
-    for step in range(1, GROUP):
-        transfer(me, lax.rem(me + step, GROUP)).start()
-
+    for step in range(8):
+        transfer(me, 8 * (1 - side) + lax.rem(me + step, 8)).start()
+    for step in range(1, 8):
+        transfer(me, 8 * side + lax.rem(me + step, 8)).start()
+
+    for load in loads[3:]:
+        load.wait()
     row = lax.rem(lax.broadcasted_iota(jnp.int32, (256, 192), 1), 64)
     below = row_start + 32 * (lax.broadcasted_iota(jnp.int32, (256, 192), 0) // 128)
     mask_m[...] = jnp.where(row >= below, m_ref[...].astype(F32), 0.0).astype(BF)
@@ -257,7 +280,7 @@
         half += dot(jnp.concatenate([main_high, edges], axis=1), w2_ref[...])
         half_high, half_low = split(half)
         full = dot(mask_m[...], jnp.concatenate([half_high, half_low, half_high], axis=0))
-        usable = dot(recv[t, 80:88, :].astype(BF), expand[...])[0:1, :]
+        usable = dot(jnp.broadcast_to(recv[t, 80:81, :], (8, 128)).astype(BF), expand[...])[0:1, :]
         for a in range(2):
             cos_part = full[128 * a : 128 * a + 64]
             sin_part = full[128 * a + 64 : 128 * a + 128]
@@ -271,7 +294,8 @@
     spectra(me)
 
     def arrive(step, carry):
-        source = lax.rem(me - step + GROUP, GROUP)
+        near = step < 8
+        source = 8 * jnp.where(near, side, 1 - side) + lax.rem(me - step + GROUP, 8)
         transfer(source, me).wait_recv()
         spectra(source)
         return carry
@@ -345,9 +369,14 @@
     halves_out = pl.pallas_call(
         kernel,
         out_shape=jax.ShapeDtypeStruct((2, 128, 128), F32),
-        in_specs=[pl.BlockSpec(memory_space=pltpu.SMEM)] + [vmem] * 7,
+        in_specs=[pl.BlockSpec(memory_space=pltpu.HBM)] * 8,
         out_specs=vmem,
         scratch_shapes=[
+            pltpu.SMEM((2,), jnp.int32),
+            pltpu.VMEM(frames.shape[1:], F32),
+            pltpu.VMEM(validity.shape, jnp.int32),
+            *[pltpu.VMEM(table.shape, BF) for table in tables_in],
+            pltpu.SemaphoreType.DMA((8,)),
             pltpu.VMEM((GROUP, 88, 128), F32),
             pltpu.VMEM((GROUP, 88, 128), F32),
             pltpu.VMEM((256, 192), BF),
@@ -363,7 +392,7 @@
             pltpu.SemaphoreType.DMA,
         ],
         compiler_params=pltpu.CompilerParams(
-            collective_id=0, has_side_effects=True, vmem_limit_bytes=40 * 1024 * 1024
+            collective_id=0, has_side_effects=True, vmem_limit_bytes=60 * 1024 * 1024
         ),
     )(anchors, frames[0], validity, *tables_in)
     parts = halves_out.reshape(2, 4, 32, 4, 32)

time: 39 us -> 34 us (0.87)
  the two profiles are of different devices: /device:TPU:12 before, /device:TPU:0 now
where the time goes in v2:
time: 34 us; the launch traced here: 33.8 us
  Pallas kernels  31.8 us (94%)
  local copies, waits for them, and re-layouts  2.05 us (6%)
    pallas_call x1, Pallas kernels, group_body(): pl.pallas_call(kernel, out_shape=jax.ShapeDtypeStruct((2, 128, 128), F32)...  31.8 us
    reshape x1, local copies, waits for them, and re-layouts, group_body(): parts = halves_out.reshape(2, 4, 32, 4, 32)  1.16 us
    transpose x1, local copies, waits for them, and re-layouts, group_body(): return parts.transpose(1, 2, 4, 0, 3).reshape(4, 32, 32, 8)  0.88 us

profile of v2, /device:TPU:0, one launch (start us, length us, event | category | flops | bytes accessed | tf_op | source)
XLA Modules:
  0.0 33.8 jit_solution(13378793820428223220)
XLA Ops:
  0.0 31.8 %shard_map.82 = f32[2,128,128]{2,1,0:T(8,128)} custom-call(s32[2]{0:T(128)} %anchor_hbm.1, f32[64,2048]{1,0:T(8,128)} %bitcast.4, s32[1,128]{1,0:T(1,128)} %v_hbm.1, bf16[256,384]{1,0:T(8,128)(2,1)} %constant.10.clone.w1_hbm, bf16[256,384]{1,0:T(8,128)(2,1)} %constant.11.clone.w2_hbm, bf16[256,192]{1,0:T(8,128)(2,1)} %constant.12.clone.m_hbm, ...), custom_call_target="tpu_custom_call" | custom-call | tf_op jit(solution)/shard_map/pallas_call | solution.py:369
  31.8 1.2 %reshape.6 = f32[2,4,32,4,32]{4,3,2,1,0:T(4,128)S(1)} reshape(f32[2,128,128]{2,1,0:T(8,128)} %shard_map.82) | data formatting | bytes 262144 | tf_op jit(solution)/shard_map/reshape | solution.py:398
  32.9 0.9 %copy.9 = f32[4,32,32,2,4]{2,4,3,1,0:T(4,128)} copy(f32[4,32,32,2,4]{2,4,1,0,3:T(4,128)S(1)} %bitcast.3) | data formatting | bytes 262144 | tf_op jit(solution)/shard_map/transpose | solution.py:399

commit v3 on v2

--- a/solution.py
+++ b/solution.py
@@ -179,7 +179,7 @@
 def kernel(
     anchor_hbm, x_hbm, v_hbm, w1_hbm, w2_hbm, m_hbm, g_hbm, h_hbm, out_ref,
     anchor_ref, x_ref, v_ref, w1_ref, w2_ref, m_ref, g_ref, h_ref, load_sem, pack, recv, mask_m, expand, sre, sim, cross, lag, plane,
-    send_sem, recv_sem, plane_send, plane_recv,
+    own, got, send_sem, recv_sem, plane_send, plane_recv,
 ):
     me = lax.axis_index("tm")
     side = me // 8
@@ -263,7 +263,7 @@
     wanted = 64 * (place // 256) + 4 * mine + which
     expand[...] = jnp.where((region == wanted) & (which < 4), 1.0, 0.0).astype(BF)
 
-    def spectra(t):
+    def operands(t):
         main_high, main_low = split(recv[t, 0:64, :])
         edge = recv[t, 64:80, :]
         edge_high = edge.astype(BF).astype(F32)
@@ -276,35 +276,50 @@
             tile = jnp.where(lane16 < 32, first, jnp.where(lane16 < 64, second, third))
             tiles.append(jnp.where(lane16 < 96, tile, 0.0))
         edges = jnp.concatenate(tiles, axis=0).astype(BF)
-        half = dot(jnp.concatenate([main_high, main_low], axis=1), w1_ref[...])
-        half += dot(jnp.concatenate([main_high, edges], axis=1), w2_ref[...])
-        half_high, half_low = split(half)
-        full = dot(mask_m[...], jnp.concatenate([half_high, half_low, half_high], axis=0))
-        usable = dot(jnp.broadcast_to(recv[t, 80:81, :], (8, 128)).astype(BF), expand[...])[0:1, :]
-        for a in range(2):
-            cos_part = full[128 * a : 128 * a + 64]
-            sin_part = full[128 * a + 64 : 128 * a + 128]
-            weight = usable[:, 256 * a : 256 * a + 256]
-            sre[t, a, :, 0:128] = (cos_part[:, 0:128] + sin_part[:, 128:256]) * weight[:, 0:128]
-            sim[t, a, :, 0:128] = (cos_part[:, 128:256] - sin_part[:, 0:128]) * weight[:, 0:128]
-            sre[t, a, :, 128:256] = cos_part[:, 256:384] * weight[:, 128:256]
-            sim[t, a, :, 128:256] = -sin_part[:, 256:384] * weight[:, 128:256]
+        return (
+            jnp.concatenate([main_high, main_low], axis=1),
+            jnp.concatenate([main_high, edges], axis=1),
+        )
+
+    def spectra(times):
+        pairs = [operands(t) for t in times]
+        halved = dot(jnp.concatenate([pair[0] for pair in pairs], axis=0), w1_ref[...])
+        halved += dot(jnp.concatenate([pair[1] for pair in pairs], axis=0), w2_ref[...])
+        flags = jnp.concatenate([recv[t, 80:81, :] for t in times] * 2, axis=0)
+        usable = dot(flags.astype(BF), expand[...])
+        for slot, t in enumerate(times):
+            half_high, half_low = split(halved[64 * slot : 64 * slot + 64])
+            full = dot(mask_m[...], jnp.concatenate([half_high, half_low, half_high], axis=0))
+            for a in range(2):
+                cos_part = full[128 * a : 128 * a + 64]
+                sin_part = full[128 * a + 64 : 128 * a + 128]
+                weight = usable[slot : slot + 1, 256 * a : 256 * a + 256]
+                main, last = weight[:, 0:128], weight[:, 128:256]
+                sre[t, a, :, 0:128] = (cos_part[:, 0:128] + sin_part[:, 128:256]) * main
+                sim[t, a, :, 0:128] = (cos_part[:, 128:256] - sin_part[:, 0:128]) * main
+                sre[t, a, :, 128:256] = cos_part[:, 256:384] * last
+                sim[t, a, :, 128:256] = -sin_part[:, 256:384] * last
+
+    def source_of(step):
+        near = step < 8
+        return 8 * jnp.where(near, side, 1 - side) + lax.rem(me - step + GROUP, 8)
 
     recv[me] = pack[mine]
-    spectra(me)
-
-    def arrive(step, carry):
-        near = step < 8
-        source = 8 * jnp.where(near, side, 1 - side) + lax.rem(me - step + GROUP, 8)
-        transfer(source, me).wait_recv()
-        spectra(source)
+    for step in range(1, 4):
+        transfer(source_of(step), me).wait_recv()
+    spectra([source_of(step) for step in range(4)])
+
+    def arrive(batch, carry):
+        sources = [source_of(4 * batch + step) for step in range(4)]
+        for source in sources:
+            transfer(source, me).wait_recv()
+        spectra(sources)
         return carry
 
-    lax.fori_loop(1, GROUP, arrive, 0)
-
-    def correlate(index, carry):
-        a = index // 8
-        start = pl.multiple_of(lax.rem(index, 8) * 8, 8)
+    lax.fori_loop(1, 4, arrive, 0)
+
+    def correlate(a, index, carry):
+        start = pl.multiple_of(index * 8, 8)
         line = lax.broadcasted_iota(jnp.int32, (8, 128), 0) + start
         column = lax.rem(lax.broadcasted_iota(jnp.int32, (8, 128), 1), 32)
         for part in range(2):
@@ -327,8 +342,6 @@
                 cross[e, a, pl.ds(start + 64, 8), lanes] = total_imag * scale
         return carry
 
-    lax.fori_loop(0, 16, correlate, 0)
-
     def back(a):
         for e in range(4):
             high, low = split(cross[e, a])
@@ -339,36 +352,46 @@
         both = dot(high, h_ref[...])
         return both[:, 0:128] + both[:, 128:256] + dot(low, h_ref[:, 0:128])
 
+    lax.fori_loop(0, 8, functools.partial(correlate, 1 - side), 0)
     plane[...] = back(1 - side)
     give = pltpu.make_async_remote_copy(
         src_ref=plane,
-        dst_ref=out_ref.at[side],
+        dst_ref=got,
         send_sem=plane_send,
         recv_sem=plane_recv,
         device_id={"tm": partner},
         device_id_type=pl.DeviceIdType.MESH,
     )
     give.start()
-    out_ref[side] = back(side)
+    lax.fori_loop(0, 8, functools.partial(correlate, side), 0)
+    own[...] = back(side)
+
+    def place_out(half, planes):
+        for b in range(4):
+            out_ref[:, 4 * half + b, :] = planes[:, 32 * b : 32 * b + 32]
+
+    for half in range(2):
+
+        @pl.when(side == half)
+        def _():
+            place_out(half, own[...])
+
     for step in range(1, GROUP):
         transfer(me, lax.rem(me + step, GROUP)).wait_send()
-    give.wait_send()
-    pltpu.make_async_remote_copy(
-        src_ref=plane,
-        dst_ref=out_ref.at[1 - side],
-        send_sem=plane_send,
-        recv_sem=plane_recv,
-        device_id={"tm": partner},
-        device_id_type=pl.DeviceIdType.MESH,
-    ).wait_recv()
+    give.wait()
+    for half in range(2):
+
+        @pl.when(side == 1 - half)
+        def _():
+            place_out(half, got[...])
 
 
 def group_body(frames, validity, anchors):
     tables_in = [jnp.asarray(table) for table in constant_tables()]
     vmem = pl.BlockSpec(memory_space=pltpu.VMEM)
-    halves_out = pl.pallas_call(
+    tiles = pl.pallas_call(
         kernel,
-        out_shape=jax.ShapeDtypeStruct((2, 128, 128), F32),
+        out_shape=jax.ShapeDtypeStruct((128, 8, 32), F32),
         in_specs=[pl.BlockSpec(memory_space=pltpu.HBM)] * 8,
         out_specs=vmem,
         scratch_shapes=[
@@ -385,7 +408,7 @@
             pltpu.VMEM((GROUP, 2, 64, 256), F32),
             pltpu.VMEM((4, 2, 128, 256), F32),
             pltpu.VMEM((128, 384), F32),
-            pltpu.VMEM((128, 128), F32),
+            *[pltpu.VMEM((128, 128), F32)] * 3,
             pltpu.SemaphoreType.DMA((GROUP,)),
             pltpu.SemaphoreType.DMA((GROUP,)),
             pltpu.SemaphoreType.DMA,
@@ -395,8 +418,7 @@
             collective_id=0, has_side_effects=True, vmem_limit_bytes=60 * 1024 * 1024
         ),
     )(anchors, frames[0], validity, *tables_in)
-    parts = halves_out.reshape(2, 4, 32, 4, 32)
-    return parts.transpose(1, 2, 4, 0, 3).reshape(4, 32, 32, 8)
+    return tiles.reshape(4, 32, 8, 32).transpose(0, 1, 3, 2)
 
 
 def solution(mesh):

time: 34 us -> 30.4 us (0.89)
  the two profiles are of different devices: /device:TPU:0 before, /device:TPU:6 now
where the time goes in v3:
time: 30.4 us; the launch traced here: 30.2 us
  Pallas kernels  28.3 us (93%)
  local copies, waits for them, and re-layouts  1.87 us (6%)
    pallas_call x1, Pallas kernels, group_body(): pl.pallas_call(kernel, out_shape=jax.ShapeDtypeStruct((128, 8, 32), F32),...  28.3 us
    unnamed x1, local copies, waits for them, and re-layouts  1.87 us

profile of v3, /device:TPU:6, one launch (start us, length us, event | category | flops | bytes accessed | tf_op | source)
XLA Modules:
  0.0 30.2 jit_solution(17848771390705284127)
XLA Ops:
  0.0 28.3 %shard_map.82 = f32[128,8,32]{2,1,0:T(8,128)} custom-call(s32[2]{0:T(128)} %anchor_hbm.1, f32[64,2048]{1,0:T(8,128)} %bitcast.5, s32[1,128]{1,0:T(1,128)} %v_hbm.1, bf16[256,384]{1,0:T(8,128)(2,1)} %constant.10.clone.w1_hbm, bf16[256,384]{1,0:T(8,128)(2,1)} %constant.11.clone.w2_hbm, bf16[256,192]{1,0:T(8,128)(2,1)} %constant.12.clone.m_hbm, ...), custom_call_target="tpu_custom_call" | custom-call | tf_op jit(solution)/shard_map/pallas_call | solution.py:392
  28.3 1.9 %copy.10 = f32[4,32,32,8]{2,3,1,0:T(8,128)} copy(f32[4,32,32,8]{2,3,1,0:T(8,128)} %bitcast.4) | data formatting | bytes 262144
